TPU v7x, 32 devices: a whole 2x2x4 slice. The times are simulated.
32 devices in a mesh: sec: 4 (over x, core), row: 4 (over z), col: 2 (over y).
Axes of the slice: x: 2, y: 2, z: 4, core: 2. Of those that a mesh axis runs over, the one named last changes fastest.
Arguments:
- amplitudes: bfloat16 [4, 2, 512, 8192], P('sec', None, 'row', 'col'), may hold values from -0.25 to 0.25, as said below
- state_energies: float32 [4, 8192], P('sec', 'col'), may hold values from 1.25 to 12
- radii_table: int32 [5], replicated, may hold values from 20 to 84, as said below
- plan: int32 [4, 2], P('sec'), may hold values from 0 to 31, as said below
- entry_r: float32 [4, 512, 512], P('sec', 'col', 'row'), may hold values from -16 to 48, as said below
- fresh_r: float32 [1, 512, 512], P(None, 'col', 'row'), may hold values from -16 to 48, as said below
Outputs:
- exit_r: float32 [2, 4, 512, 512], P(None, 'sec', 'col', 'row')
Inputs may be any that keep to these rules, and one draw needn't show every extreme that they name: Each sector's outer-boundary amplitudes are correlated with its inner-boundary ones. `radii_table`: strictly increasing; consecutive radii differ by 4 to 16; the first is at least 20 and the last equals 84. plan[s, t] equals plan[s-1, t-1] for s, t >= 1. `entry_r`: symmetric positive definite, every eigenvalue at least 0.5. `fresh_r`: symmetric positive definite, every eigenvalue at least 0.5.
All inputs are finite; a program needn't handle non-finite values.
Results may differ from a plain program's by a relative error of at most 0.0016.
Values may be sent and summed in bfloat16 or wider, within the bound.
A program may use at most 64 MiB of HBM per device.

v0:
```python
import jax
import jax.numpy as jnp
from jax import lax
from jax.sharding import PartitionSpec as P

ENERGIES = 32
TICKS = 2


def shifted_2(block, axis, distance):
    devices = range(lax.axis_size(axis))
    route = [(i - distance, i) for i in devices if i - distance in devices]
    return lax.ppermute(block, axis, route)


def contract(left_rows, right_rows, paired_panels, right_panel):
    contraction = (((1,), (1,)), ((), ()))
    paired_out = lax.dot_general(
        left_rows, paired_panels, contraction, preferred_element_type=jnp.float32
    )
    right_out = lax.dot_general(
        right_rows, right_panel, contraction, preferred_element_type=jnp.float32
    )
    return jnp.concatenate([paired_out, right_out], 1)


def local(amplitudes, state_energies, radii_table, plan, entry_r, fresh_r):
    sec_index = lax.axis_index("sec")
    row_index = lax.axis_index("row")
    col_index = lax.axis_index("col")
    col_count = lax.axis_size("col")
    local_panels = amplitudes[0]
    col_block = local_panels.shape[1]
    all_panels = lax.all_gather(local_panels, "row", axis=1, tiled=True)
    channels = all_panels.shape[1]
    row_block = channels // col_count
    paired_panels = local_panels.reshape(2 * col_block, local_panels.shape[2])
    bounds = lax.dynamic_slice_in_dim(radii_table, sec_index, 2)
    sector_width = (bounds[1] - bounds[0]).astype(jnp.float32)
    levels = state_energies[0]
    boundary = entry_r[0]
    results = []
    for period in range(TICKS):
        energy = plan[0, period].astype(jnp.float32) / ENERGIES
        weight = 8.0 / (sector_width * (levels - energy))
        scaled = (all_panels.astype(jnp.float32) * weight).astype(jnp.bfloat16)
        columns = lax.psum(contract(scaled[0], scaled[1], paired_panels, local_panels[1]), "col")
        r_columns = lax.all_gather(boundary, "col", axis=0, tiled=True)
        full_system, full_cross = (
            lax.all_gather(columns[:, :col_block] + r_columns, "row", axis=1, tiled=True),
            lax.all_gather(columns[:, col_block : 2 * col_block], "row", axis=1, tiled=True),
        )
        green_tile = lax.dynamic_slice_in_dim(
            columns[:, 2 * col_block :], col_index * row_block, row_block, 0
        )
        factor = jnp.linalg.cholesky(full_system)
        needed = jnp.concatenate(
            [
                lax.dynamic_slice_in_dim(full_cross, col_index * row_block, row_block, 1),
                lax.dynamic_slice_in_dim(full_cross, row_index * col_block, col_block, 1),
            ],
            1,
        )
        solved = jax.scipy.linalg.solve_triangular(factor, needed, lower=True)
        exit_tile = green_tile - jnp.dot(
            solved[:, :row_block].T, solved[:, row_block:], precision=lax.Precision.HIGHEST
        )
        results.append(exit_tile)
        if period + 1 < TICKS:
            shifted = shifted_2(exit_tile, "sec", 1)
            boundary = jnp.where(sec_index == 0, fresh_r[period], shifted)
    return jnp.stack(results, 0)[:, None]


def solution(mesh):
    placed = (
        P("sec", None, "row", "col"),
        P("sec", "col"),
        P(),
        P("sec", None),
        P("sec", "col", "row"),
        P(None, "col", "row"),
    )
    return jax.shard_map(
        local, mesh=mesh, in_specs=placed, out_specs=P(None, "sec", "col", "row"), check_vma=False
    )
```

profile of v0, /device:TPU:29, one launch (start us, length us, event | category | flops | bytes accessed | tf_op | source)
XLA Modules:
  0.0 583.9 jit_solution(4339053105319797637)
XLA Ops:
  13.2 143.7 %all-gather.16.cloned.1.call-done = bf16[1,2,512,4096]{3,2,1,0:T(8,128)(2,1)} async-done(((bf16[1,2,128,4096]{3,2,1,0:T(8,128)(2,1)}), bf16[1,2,512,4096]{3,2,1,0:T(8,128)(2,1)}) %all-gather.16.cloned.1.call-update) | async-done | bytes 8388624 | tf_op jit(solution)/shard_map/all_gather | solution.py:34
  156.9 6.6 %fusion = (bf16[2,512,4096]{2,1,0:T(8,128)(2,1)S(1)}, bf16[2,512,4096]{2,1,0:T(8,128)(2,1)S(1)}) fusion(bf16[1,2,512,4096]{3,2,1,0:T(8,128)(2,1)} %all-gather.16.cloned.1.call-done, f32[4096]{0:T(1024)S(1)} %bitcast.137, f32[4096]{0:T(1024)S(1)} %bitcast.138), kind=kLoop, calls=%fused_computation.6 | loop fusion | flops 20971520 | bytes 25198592 | tf_op jit(solution)/shard_map/convert_element_type | solution.py:46
  163.6 1.5 fusion.2
  167.7 1.5 fusion.4
  170.7 5.3 all-gather.1
  175.9 46.3 %all-reduce.4.cloned.1.call-done = (f32[512,384]{0,1:T(8,128)}, f32[512,384]{0,1:T(8,128)}) async-done(((f32[512,384]{0,1:T(8,128)}, f32[512,384]{0,1:T(8,128)}), (f32[512,384]{0,1:T(8,128)}, f32[512,384]{0,1:T(8,128)})) %all-reduce.4.cloned.1.call-update) | async-done | bytes 1572880 | tf_op jit(solution)/shard_map/psum | solution.py:47
  222.2 2.0 fusion.100
  225.0 26.9 %all-gather.8.cloned.1.call-done = f32[512,512]{0,1:T(8,128)} async-done(((f32[512,128]{0,1:T(8,128)}), f32[512,512]{0,1:T(8,128)}) %all-gather.8.cloned.1.call-update) | async-done | bytes 1048592 | tf_op jit(solution)/shard_map/all_gather | solution.py:50
  252.0 1.6 copy.8
  255.0 11.7 %cholesky.286 = f32[128,128]{1,0:T(8,128)S(1)} custom-call(f32[128,128]{1,0:T(8,128)S(1)} %cholesky.426), custom_call_target="Cholesky" | custom-call | tf_op jit(solution)/shard_map/jit(cholesky)/cholesky | solution.py:56
  266.9 9.8 %custom-call.27 = f32[1,128,128]{1,2,0:T(8,128)S(1)} custom-call(f32[1,128,128]{2,1,0:T(8,128)S(1)} %get-tuple-element.72), custom_call_target="InvertDiagBlocksLowerTriangular" | custom-call | tf_op jit(solution)/shard_map/jit(cholesky)/cholesky | solution.py:56
  277.4 11.7 %cholesky.305 = f32[128,128]{1,0:T(8,128)S(1)} custom-call(f32[128,128]{1,0:T(8,128)S(1)} %cholesky.430), custom_call_target="Cholesky" | custom-call | tf_op jit(solution)/shard_map/jit(cholesky)/cholesky | solution.py:56
  290.5 10.0 %custom-call.28 = f32[1,128,128]{1,2,0:T(8,128)S(1)} custom-call(f32[1,128,128]{2,1,0:T(8,128)S(1)} %get-tuple-element.69), custom_call_target="InvertDiagBlocksLowerTriangular" | custom-call | tf_op jit(solution)/shard_map/jit(cholesky)/cholesky | solution.py:56
  301.1 11.7 %cholesky.326 = f32[128,128]{1,0:T(8,128)S(1)} custom-call(f32[128,128]{1,0:T(8,128)S(1)} %cholesky.435), custom_call_target="Cholesky" | custom-call | tf_op jit(solution)/shard_map/jit(cholesky)/cholesky | solution.py:56
  313.6 9.8 %custom-call.29 = f32[1,128,128]{1,2,0:T(8,128)S(1)} custom-call(f32[1,128,128]{2,1,0:T(8,128)S(1)} %get-tuple-element.66), custom_call_target="InvertDiagBlocksLowerTriangular" | custom-call | tf_op jit(solution)/shard_map/jit(cholesky)/cholesky | solution.py:56
  324.0 11.7 %cholesky.343 = f32[128,128]{1,0:T(8,128)S(1)} custom-call(f32[128,128]{1,0:T(8,128)S(1)} %convolution_subtract_fusion.13), custom_call_target="Cholesky" | custom-call | tf_op jit(solution)/shard_map/jit(cholesky)/cholesky | solution.py:56
  339.5 8.0 %while.4 = (s32[]{:T(128)}, f32[512,512]{1,0:T(8,128)S(1)}, s32[4,2]{0,1:T(2,128)S(1)}, f32[4,128,128]{2,1,0:T(8,128)S(1)}, s32[]{:T(128)}) while((s32[]{:T(128)}, f32[512,512]{1,0:T(8,128)S(1)}, s32[4,2]{0,1:T(2,128)S(1)}, f32[4,128,128]{2,1,0:T(8,128)S(1)}, s32[]{:T(128)}) %tuple.59), condition=%wide.while_cond, body=%wide.while_body.sunk | while | flops 2 | bytes 131181 | solution.py:64
  347.5 39.3 %custom-call.30 = f32[4,128,128]{1,2,0:T(8,128)S(1)} custom-call(f32[4,128,128]{2,1,0:T(8,128)S(1)} %get-tuple-element.21), custom_call_target="InvertDiagBlocksLowerTriangular" | custom-call | tf_op jit(solution)/shard_map/jit(_solve_triangular)/triangular_solve | solution.py:64
  393.6 3.5 collective-permute-start
  397.3 1.8 collective-permute-done
  399.1 4.5 all_gather.25
  405.1 29.0 %all-gather.12.cloned.1.call-done = f32[512,512]{0,1:T(8,128)} async-done(((f32[512,128]{0,1:T(8,128)}), f32[512,512]{0,1:T(8,128)}) %all-gather.12.cloned.1.call-update) | async-done | bytes 1048592 | tf_op jit(solution)/shard_map/all_gather | solution.py:50
  434.1 1.6 copy.11
  437.1 11.7 %cholesky.358 = f32[128,128]{1,0:T(8,128)S(1)} custom-call(f32[128,128]{1,0:T(8,128)S(1)} %cholesky.439), custom_call_target="Cholesky" | custom-call | tf_op jit(solution)/shard_map/jit(cholesky)/cholesky | solution.py:56
  449.0 9.8 %custom-call.31 = f32[1,128,128]{1,2,0:T(8,128)S(1)} custom-call(f32[1,128,128]{2,1,0:T(8,128)S(1)} %get-tuple-element.62), custom_call_target="InvertDiagBlocksLowerTriangular" | custom-call | tf_op jit(solution)/shard_map/jit(cholesky)/cholesky | solution.py:56
  459.5 11.7 %cholesky.377 = f32[128,128]{1,0:T(8,128)S(1)} custom-call(f32[128,128]{1,0:T(8,128)S(1)} %cholesky.443), custom_call_target="Cholesky" | custom-call | tf_op jit(solution)/shard_map/jit(cholesky)/cholesky | solution.py:56
  472.6 10.0 %custom-call.32 = f32[1,128,128]{1,2,0:T(8,128)S(1)} custom-call(f32[1,128,128]{2,1,0:T(8,128)S(1)} %get-tuple-element.59), custom_call_target="InvertDiagBlocksLowerTriangular" | custom-call | tf_op jit(solution)/shard_map/jit(cholesky)/cholesky | solution.py:56
  483.3 11.7 %cholesky.398 = f32[128,128]{1,0:T(8,128)S(1)} custom-call(f32[128,128]{1,0:T(8,128)S(1)} %cholesky.448), custom_call_target="Cholesky" | custom-call | tf_op jit(solution)/shard_map/jit(cholesky)/cholesky | solution.py:56
  495.7 9.8 %custom-call.33 = f32[1,128,128]{1,2,0:T(8,128)S(1)} custom-call(f32[1,128,128]{2,1,0:T(8,128)S(1)} %get-tuple-element.56), custom_call_target="InvertDiagBlocksLowerTriangular" | custom-call | tf_op jit(solution)/shard_map/jit(cholesky)/cholesky | solution.py:56
  506.1 11.7 %cholesky.415 = f32[128,128]{1,0:T(8,128)S(1)} custom-call(f32[128,128]{1,0:T(8,128)S(1)} %convolution_subtract_fusion.12), custom_call_target="Cholesky" | custom-call | tf_op jit(solution)/shard_map/jit(cholesky)/cholesky | solution.py:56
  521.5 8.1 %while.5 = (s32[]{:T(128)}, f32[512,512]{1,0:T(8,128)S(1)}, s32[4,2]{0,1:T(2,128)S(1)}, f32[4,128,128]{2,1,0:T(8,128)S(1)}, s32[]{:T(128)}) while((s32[]{:T(128)}, f32[512,512]{1,0:T(8,128)S(1)}, s32[4,2]{0,1:T(2,128)S(1)}, f32[4,128,128]{2,1,0:T(8,128)S(1)}, s32[]{:T(128)}) %tuple.78), condition=%wide.while_cond.clone, body=%wide.while_body.clone.sunk | while | flops 2 | bytes 131181 | solution.py:64
  529.6 39.3 %custom-call.34 = f32[4,128,128]{1,2,0:T(8,128)S(1)} custom-call(f32[4,128,128]{2,1,0:T(8,128)S(1)} %get-tuple-element.22), custom_call_target="InvertDiagBlocksLowerTriangular" | custom-call | tf_op jit(solution)/shard_map/jit(_solve_triangular)/triangular_solve | solution.py:64
  (125 shorter events, 54.5 us)
Async XLA Ops:
  6.5 150.4 %all-gather.16.cloned.1.call-start = ((), (), s32[]{:S(2)}) async-start(), calls=%async_computation.4 | async-start | bytes 10485760 | tf_op jit(solution)/shard_map/all_gather | solution.py:34
  7.3 215.0 %all-reduce.4.cloned.1.call-start = ((), (), s32[]{:S(2)}) async-start(), calls=%async_computation.5 | async-start | bytes 3145728 | tf_op jit(solution)/shard_map/psum | solution.py:47
  156.9 6.6 %copy-start = (bf16[1,2,128,4096]{3,2,1,0:T(8,128)(2,1)S(1)}, bf16[1,2,128,4096]{3,2,1,0:T(8,128)(2,1)}, u32[]{:S(2)}) copy-start(bf16[1,2,128,4096]{3,2,1,0:T(8,128)(2,1)} %param.9) | copy-start | bytes 6291460
  167.7 2.9 copy-start.2
  170.5 81.5 %all-gather.8.cloned.1.call-start = ((), (), s32[]{:S(2)}) async-start(), calls=%async_computation | async-start | bytes 1310720 | tf_op jit(solution)/shard_map/all_gather | solution.py:50
  224.2 162.6 %all-gather.10.cloned.1.call-start = ((), (), s32[]{:S(2)}) async-start(), calls=%async_computation.1 | async-start | bytes 1310720 | tf_op jit(solution)/shard_map/all_gather | solution.py:51
  224.8 209.3 %all-gather.12.cloned.1.call-start = ((), (), s32[]{:S(2)}) async-start(), calls=%async_computation.2 | async-start | bytes 1310720 | tf_op jit(solution)/shard_map/all_gather | solution.py:50
  300.4 96.7 %copy-start.3 = (f32[1,256,128]{2,1,0:T(8,128)S(1)}, f32[1,256,128]{2,1,0:T(8,128)}, u32[]{:S(2)}) copy-start(f32[1,256,128]{2,1,0:T(8,128)} %param.14) | copy-start | bytes 393220
  312.8 90.7 %copy-start.1 = (f32[512,384]{0,1:T(8,128)S(1)}, f32[512,384]{0,1:T(8,128)}, u32[]{:S(2)}) copy-start(f32[512,384]{0,1:T(8,128)} %get-tuple-element.39) | copy-start | bytes 2359300
  393.6 5.4 collective-permute-start
  404.5 164.5 %all-gather.14.cloned.1.call-start = ((), (), s32[]{:S(2)}) async-start(), calls=%async_computation.3 | async-start | bytes 1310720 | tf_op jit(solution)/shard_map/all_gather | solution.py:51
Sparse Core Ops, SparseCore 0:
  8.9 147.9 all-gather.15
  170.6 51.5 all-reduce.3
  224.4 27.5 all-gather.7
  253.5 27.4 all-gather.9
  404.6 29.4 all-gather.11
  435.6 27.4 all-gather.13
where the time goes:
time: 592 us; the launch traced here: 584 us
  other arithmetic  253 us (43%)
  waiting for transfers between devices  249 us (42%)
  local copies, waits for them, and re-layouts  27.2 us (5%)
  between operations  22 us (4%)
  matrix products  18.6 us (3%)
  blocking collectives  9.76 us (2%)
    another operation x30, other arithmetic, local(): factor = jnp.linalg.cholesky(full_system)  159 us
    all_gather x1, waiting for transfers between devices, local(): all_panels = lax.all_gather(local_panels, 'row', axis=1, tiled=True)  144 us
    another operation x7, other arithmetic, local(): solved = jax.scipy.linalg.solve_triangular(factor, needed, lower=True)  79.6 us
    all_gather x2, waiting for transfers between devices, local(): lax.all_gather(columns[:, :col_block] + r_columns, 'row', axis=1, tiled=T...  56 us
    psum x1, waiting for transfers between devices, local(): lax.psum(contract(scaled[0], scaled[1], paired_panels, local_panels[1]),...  46.3 us
    another operation x27, local copies, waits for them, and re-layouts, local(): solved = jax.scipy.linalg.solve_triangular(factor, needed, lower=True)  16 us
  transfers between devices with their start and end apart: 7, of which 5 were waited for; matrix products, arithmetic and copies ran while one was open for 46% of the time, Pallas kernels for 0%

commit v1 on v0

v1 whole, which is shorter than its diff:
```python
import functools
import jax
import jax.numpy as jnp
from jax import lax
from jax.experimental import pallas as pl
from jax.experimental.pallas import tpu as pltpu
from jax.sharding import PartitionSpec as P

ENERGIES = 32
TICKS = 2
BLOCK = 128
SUB = 8
HIGHEST = lax.Precision.HIGHEST


def shifted_2(block, axis, distance):
    devices = range(lax.axis_size(axis))
    route = [(i - distance, i) for i in devices if i - distance in devices]
    return lax.ppermute(block, axis, route)


def inverse_factor(block):
    size = block.shape[0]
    groups = size // SUB
    sub_rows = lax.broadcasted_iota(jnp.int32, (SUB, size), 0)
    lanes = lax.broadcasted_iota(jnp.int32, (SUB, size), 1)
    left = [block[SUB * g : SUB * (g + 1), :] for g in range(groups)]
    right = [jnp.where(lanes == sub_rows + SUB * g, 1.0, 0.0) for g in range(groups)]
    done = []
    for g in range(groups):
        base = SUB * g
        u, v = left[g], right[g]
        cols = [jnp.broadcast_to(u[:, base + q : base + q + 1], (SUB, size)) for q in range(SUB)]
        scale = jnp.zeros((SUB, size), jnp.float32)
        for p in range(SUB):
            pivot = cols[p][p : p + 1, :]
            scale = jnp.where(sub_rows == p, pivot, scale)
            if p + 1 < SUB:
                f = jnp.where(sub_rows > p, cols[p] / pivot, 0.0)
                u = u - f * u[p : p + 1, :]
                v = v - f * v[p : p + 1, :]
                for q in range(p + 1, SUB):
                    cols[q] = cols[q] - f * cols[q][p : p + 1, :]
        scale = lax.rsqrt(scale)
        u = u * scale
        v = v * scale
        done.append(v)
        if g + 1 < groups:
            turned = u.T
            for h in range(g + 1, groups):
                for q in range(SUB):
                    c = jnp.broadcast_to(turned[SUB * h : SUB * (h + 1), q : q + 1], (SUB, size))
                    left[h] = left[h] - c * u[q : q + 1, :]
                    right[h] = right[h] - c * v[q : q + 1, :]
    return jnp.concatenate(done, 0)


def eliminate_kernel(ll_ref, lr_ref, rr_ref, entry_ref, out_ref, work):
    n = ll_ref.shape[0]
    blocks = n // BLOCK
    work[:n, :n] = ll_ref[...] + entry_ref[...]
    work[:n, n:] = lr_ref[...]
    work[n:, n:] = rr_ref[...]
    for k in range(blocks):
        lo, hi = k * BLOCK, (k + 1) * BLOCK
        factor = inverse_factor(work[lo:hi, lo:hi])
        solved = jnp.dot(
            factor, work[lo:hi, hi:], precision=HIGHEST, preferred_element_type=jnp.float32
        )
        for i in range(hi, 2 * n, BLOCK):
            work[i : i + BLOCK, i:] -= lax.dot_general(
                solved[:, i - hi : i - hi + BLOCK],
                solved[:, i - hi :],
                (((0,), (0,)), ((), ())),
                precision=HIGHEST,
                preferred_element_type=jnp.float32,
            )
    for i in range(blocks):
        for j in range(i, blocks):
            tile = work[n + i * BLOCK : n + (i + 1) * BLOCK, n + j * BLOCK : n + (j + 1) * BLOCK]
            out_ref[i * BLOCK : (i + 1) * BLOCK, j * BLOCK : (j + 1) * BLOCK] = tile
            if j > i:
                out_ref[j * BLOCK : (j + 1) * BLOCK, i * BLOCK : (i + 1) * BLOCK] = tile.T


def eliminate(ll, lr, rr, entry):
    n = ll.shape[0]
    return pl.pallas_call(
        eliminate_kernel,
        out_shape=jax.ShapeDtypeStruct((n, n), jnp.float32),
        in_specs=[pl.BlockSpec(memory_space=pltpu.VMEM)] * 4,
        out_specs=pl.BlockSpec(memory_space=pltpu.VMEM),
        scratch_shapes=[pltpu.VMEM((2 * n, 2 * n), jnp.float32)],
        compiler_params=pltpu.CompilerParams(vmem_limit_bytes=32 * 1024 * 1024),
        cost_estimate=pl.CostEstimate(
            flops=200 * n * n * n, bytes_accessed=20 * n * n, transcendentals=0
        ),
        name="eliminate",
    )(ll, lr, rr, entry)


def local(amplitudes, state_energies, radii_table, plan, entry_r, fresh_r):
    sec_index = lax.axis_index("sec")
    row_index = lax.axis_index("row")
    col_index = lax.axis_index("col")
    row_count = lax.axis_size("row")
    panels = lax.all_to_all(amplitudes[0], "row", split_axis=2, concat_axis=1, tiled=True)
    channels, states = panels.shape[1:]
    row_block, col_block = entry_r.shape[1:]
    levels = lax.dynamic_slice_in_dim(state_energies[0], row_index * states, states)
    bounds = lax.dynamic_slice_in_dim(radii_table, sec_index, 2)
    sector_width = (bounds[1] - bounds[0]).astype(jnp.float32)
    contraction = (((1,), (1,)), ((), ()))
    zeros = jnp.zeros((channels, channels), jnp.float32)
    sums = []
    for period in range(TICKS):
        energy = plan[0, period].astype(jnp.float32) / ENERGIES
        weight = 8.0 / (sector_width * (levels - energy))
        scaled = (panels.astype(jnp.float32) * weight).astype(jnp.bfloat16)
        ll = lax.dot_general(scaled[0], panels[0], contraction, preferred_element_type=jnp.float32)
        lr = lax.dot_general(scaled[0], panels[1], contraction, preferred_element_type=jnp.float32)
        rr = lax.dot_general(scaled[1], panels[1], contraction, preferred_element_type=jnp.float32)
        if period == 0:
            tile = entry_r[0]
        else:
            tile = jnp.where(sec_index == 0, fresh_r[period - 1], 0.0)
        place = (col_index * row_block, row_index * col_block)
        tile = tile + lax.dynamic_slice(ll, place, (row_block, col_block))
        ll = lax.dynamic_update_slice(ll, tile, place)
        sums.append(lax.psum(jnp.stack([ll, lr, rr]), ("row", "col")))
    boundary = zeros
    results = []
    for period in range(TICKS):
        ll, lr, rr = sums[period]
        exit_full = eliminate(ll, lr, rr, boundary)
        results.append(
            lax.dynamic_slice(
                exit_full, (col_index * row_block, row_index * col_block), (row_block, col_block)
            )
        )
        if period + 1 < TICKS:
            boundary = shifted_2(exit_full, "sec", 1)
    return jnp.stack(results, 0)[:, None]


def solution(mesh):
    placed = (
        P("sec", None, "row", "col"),
        P("sec", "col"),
        P(),
        P("sec", None),
        P("sec", "col", "row"),
        P(None, "col", "row"),
    )
    return jax.shard_map(
        local, mesh=mesh, in_specs=placed, out_specs=P(None, "sec", "col", "row"), check_vma=False
    )
```

time: 592 us -> 389 us (0.66)
  other arithmetic: 253 us -> 8.51 us
  Pallas kernels: 0 us -> 54.1 us
  waiting for transfers between devices: 249 us -> 265 us
  matrix products: 18.6 us -> 8.1 us
  blocking collectives: 9.76 us -> 0 us
    another operation x37 -> x2, other arithmetic: 238 us -> 3.99 us  [local(): sums.append(lax.psum(jnp.stack([ll, lr, rr]), ('row', 'col')))]
    all_gather x5 -> x0, waiting for transfers between devices: 200 us -> none  [the longest x1 144 us: local(): all_panels = lax.all_gather(local_panels, 'row', axis=1, tiled=True)]
    psum x1, waiting for transfers between devices: 46.3 us -> 213 us  [local(): sums.append(lax.psum(jnp.stack([ll, lr, rr]), ('row', 'col')))]
    pallas_call x0 -> x2, Pallas kernels: none -> 54.1 us  [eliminate(): pl.pallas_call(eliminate_kernel, out_shape=jax.ShapeDtypeStruct((n, n), j...]
    all_to_all x0 -> x1, waiting for transfers between devices: none -> 40.7 us  [local(): lax.all_to_all(amplitudes[0], 'row', split_axis=2, concat_axis=1, tiled=T...]
    another operation x35 -> x4, local copies, waits for them, and re-layouts: 16.3 us -> 2.52 us  [the longest x2 2.47 us: local(): ll, lr, rr = sums[period]]
    another operation x26 -> x0, matrix products: 11.8 us -> none  [the longest x14 8.05 us: local(): solved = jax.scipy.linalg.solve_triangular(factor, needed, lower=True)]
    all_gather x2 -> x0, blocking collectives: 9.76 us -> none  [local(): r_columns = lax.all_gather(boundary, 'col', axis=0, tiled=True)]
  transfers between devices with their start and end apart: 7 -> 3, of which waited for: 5 -> 3; matrix products, arithmetic and copies ran while one was open for 46% -> 1% of each run, Pallas kernels for 0% -> 0%
where the time goes in v1:
time: 389 us; the launch traced here: 382 us
  waiting for transfers between devices  265 us (68%)
  Pallas kernels  54.1 us (14%)
  local copies, waits for them, and re-layouts  21.5 us (6%)
  between operations  16.4 us (4%)
  other arithmetic  8.51 us (2%)
  starting transfers between devices  8.5 us (2%)
  matrix products  8.1 us (2%)
    psum x1, waiting for transfers between devices, local(): sums.append(lax.psum(jnp.stack([ll, lr, rr]), ('row', 'col')))  213 us
    pallas_call x2, Pallas kernels, eliminate(): pl.pallas_call(eliminate_kernel, out_shape=jax.ShapeDtypeStruct((n, n), j...  54.1 us
    all_to_all x1, waiting for transfers between devices, local(): lax.all_to_all(amplitudes[0], 'row', split_axis=2, concat_axis=1, tiled=T...  40.7 us
    ppermute x1, waiting for transfers between devices, shifted_2(): return lax.ppermute(block, axis, route)  11 us
  transfers between devices with their start and end apart: 3, of which 3 were waited for; matrix products, arithmetic and copies ran while one was open for 1% of the time, Pallas kernels for 0%

profile of v1, /device:TPU:29, one launch (start us, length us, event | category | flops | bytes accessed | tf_op | source)
XLA Modules:
  0.0 381.8 jit_solution(410175426765952655)
XLA Ops:
  6.5 6.2 %copy.11 = bf16[1,2,128,4096]{2,1,3,0:T(2,128)(2,1)} copy(bf16[1,2,128,4096]{3,2,1,0:T(8,128)(2,1)} %param.6) | data formatting | bytes 4194304 | tf_op args[0]
  12.7 4.7 %all-to-all-start = ((bf16[2,128,4096]{1,0,2:T(2,128)(2,1)}), bf16[2,128,4096]{1,0,2:T(2,128)(2,1)}, u32[]{:S(2)}, u32[]{:S(2)}) async-start(bf16[2,128,4096]{1,0,2:T(2,128)(2,1)} %bitcast), calls=%async_computation | async-start | bytes 4194304 | tf_op jit(solution)/shard_map/all_to_all | solution.py:107
  17.4 0.1 dynamic_slice.18
  17.4 0.6 fusion.6
  19.4 0.6 fusion.5
  21.3 0.7 multiply_divide_fusion.1
  22.0 40.7 %all-to-all-done = bf16[2,128,4096]{1,0,2:T(2,128)(2,1)} async-done(((bf16[2,128,4096]{1,0,2:T(2,128)(2,1)}), bf16[2,128,4096]{1,0,2:T(2,128)(2,1)}, u32[]{:S(2)}, u32[]{:S(2)}) %all-to-all-start) | async-done | bytes 2097184 | tf_op jit(solution)/shard_map/all_to_all | solution.py:107
  62.7 1.9 copy.12
  64.5 3.1 copy.13
  67.7 1.1 fusion.4
  68.8 2.3 copy.15
  71.1 3.0 fusion
  74.1 1.7 convolution_bitcast_fusion.2
  75.9 1.7 convolution_bitcast_fusion.3
  77.6 1.5 copy.14
  79.1 2.4 fusion.2
  81.6 0.7 fusion.3
  82.3 0.7 convolution_bitcast_fusion.1
  83.1 0.7 convolution_bitcast_fusion
  84.1 1.0 copy-done.5
  85.1 0.3 copy-done.6
  85.4 2.0 pad_maximum_fusion
  87.4 2.0 pad_maximum_fusion.1
  89.4 213.0 %all-reduce.3.cloned.1.call-done = (f32[3,512,512]{2,1,0:T(8,128)}, f32[3,512,512]{2,1,0:T(8,128)}) async-done(((f32[3,512,512]{2,1,0:T(8,128)}, f32[3,512,512]{2,1,0:T(8,128)}), (f32[3,512,512]{2,1,0:T(8,128)}, f32[3,512,512]{2,1,0:T(8,128)})) %all-reduce.3.cloned.1.call-update) | async-done | bytes 6291472 | tf_op jit(solution)/shard_map/psum | solution.py:130
  302.4 2.2 slice_bitcast_fusion.6
  304.6 0.1 broadcast_in_dim.12.entry_ref
  304.7 27.1 %eliminate.2 = f32[512,512]{1,0:T(8,128)S(1)} custom-call(f32[512,512]{1,0:T(8,128)S(1)} %get-tuple-element.11.ll_ref, f32[512,512]{1,0:T(8,128)S(1)} %get-tuple-element.10.lr_ref, f32[512,512]{1,0:T(8,128)S(1)} %get-tuple-element.9.rr_ref, f32[512,512]{1,0:T(8,128)S(1)} %broadcast_in_dim.12.entry_ref), custom_call_target="tpu_custom_call" | custom-call | flops 26843545600 | bytes 5242880 | tf_op jit(solution)/shard_map/eliminate/pallas_call | solution.py:88
  331.8 3.8 %collective-permute-start = (f32[512,512]{1,0:T(8,128)S(1)}, f32[512,512]{1,0:T(8,128)S(1)}, u32[]{:S(2)}, u32[]{:S(2)}) collective-permute-start(f32[512,512]{1,0:T(8,128)S(1)} %eliminate.2), channel_id=1, source_target_pairs={{0,8},{8,16},{16,24},{1,9},{9,17},{17,25},{2,10},{10,18},{18,26},{... | collective-permute-start | bytes 3145736 | tf_op jit(solution)/shard_map/ppermute | solution.py:19
  335.7 0.3 slice_bitcast_fusion
  336.0 11.0 %collective-permute-done.entry_ref = f32[512,512]{1,0:T(8,128)S(1)} collective-permute-done((f32[512,512]{1,0:T(8,128)S(1)}, f32[512,512]{1,0:T(8,128)S(1)}, u32[]{:S(2)}, u32[]{:S(2)}) %collective-permute-start) | collective-permute-done | bytes 1048608 | tf_op jit(solution)/shard_map/ppermute | solution.py:19
  347.0 27.0 %eliminate.3 = f32[512,512]{1,0:T(8,128)S(1)} custom-call(f32[512,512]{1,0:T(8,128)S(1)} %get-tuple-element.14.ll_ref, f32[512,512]{1,0:T(8,128)S(1)} %get-tuple-element.13.lr_ref, f32[512,512]{1,0:T(8,128)S(1)} %get-tuple-element.12.rr_ref, f32[512,512]{1,0:T(8,128)S(1)} %collective-permute-done.entry_ref), custom_call_target="tpu_custom_call" | custom-call | flops 26843545600 | bytes 5242880 | tf_op jit(solution)/shard_map/eliminate/pallas_call | solution.py:88
  374.1 0.7 maximum_bitcast_fusion
  (27 shorter events, 0.3 us)
Async XLA Ops:
  12.7 4.7 %copy-start.10 = (s32[5]{0:T(128)S(1)}, s32[5]{0:T(128)}, u32[]{:S(2)}) copy-start(s32[5]{0:T(128)} %param.8) | copy-start | bytes 64
  12.7 6.7 %copy-start.9 = (s32[1,2]{1,0:T(1,128)S(1)}, s32[1,2]{1,0:T(1,128)}, u32[]{:S(2)}) copy-start(s32[1,2]{1,0:T(1,128)} %param.9) | copy-start | bytes 28
  12.7 50.0 %all-to-all-start = ((bf16[2,128,4096]{1,0,2:T(2,128)(2,1)}), bf16[2,128,4096]{1,0,2:T(2,128)(2,1)}, u32[]{:S(2)}, u32[]{:S(2)}) async-start(bf16[2,128,4096]{1,0,2:T(2,128)(2,1)} %bitcast), calls=%async_computation | async-start | bytes 4194304 | tf_op jit(solution)/shard_map/all_to_all | solution.py:107
  17.4 285.1 %all-reduce.3.cloned.1.call-start = ((), (), s32[]{:S(2)}) async-start(), calls=%async_computation.1 | async-start | bytes 12582912 | tf_op jit(solution)/shard_map/psum | solution.py:130
  71.1 3.1 copy-start.2
  74.1 3.5 copy-start.1
  79.1 2.5 copy-start.4
  79.1 3.2 copy-start.3
  83.1 0.9 copy-start.7
  83.1 1.0 copy-start.8
  83.8 1.3 copy-start.5
  83.8 1.6 copy-start.6
  304.7 31.0 %copy-start = (f32[3,512,512]{2,1,0:T(8,128)S(1)}, f32[3,512,512]{2,1,0:T(8,128)}, u32[]{:S(2)}) copy-start(f32[3,512,512]{2,1,0:T(8,128)} %get-tuple-element.5) | copy-start | bytes 9437188
  331.8 15.2 %collective-permute-start = (f32[512,512]{1,0:T(8,128)S(1)}, f32[512,512]{1,0:T(8,128)S(1)}, u32[]{:S(2)}, u32[]{:S(2)}) collective-permute-start(f32[512,512]{1,0:T(8,128)S(1)} %eliminate.2), channel_id=1, source_target_pairs={{0,8},{8,16},{16,24},{1,9},{9,17},{17,25},{2,10},{10,18},{18,26},{... | collective-permute-start | bytes 3145736 | tf_op jit(solution)/shard_map/ppermute | solution.py:19
Sparse Core Ops, SparseCore 0:
  89.5 212.8 all-reduce.2
